TPU v7x, 32 devices: a whole 2x2x4 slice. The times are simulated.
32 devices in a mesh: blk: 8 (over z, x), grp: 4 (over y, core).
Axes of the slice: x: 2, y: 2, z: 4, core: 2. Of those that a mesh axis runs over, the one named last changes fastest.
Arguments:
- factors: bfloat16 [2, 3072, 3072], P(None, 'blk', 'grp'), may hold values from -0.109375 to 0.109375
- lower_inverse: float32 [2, 3072, 128], P(None, 'blk'), may hold values from -1 to 2
- upper_inverse: float32 [2, 3072, 128], P(None, 'blk'), may hold values from -1 to 2
- right_side: float32 [2, 3072, 512], P(None, 'blk', 'grp'), may hold values from -6 to 6
Outputs:
- solution: float32 [2, 3072, 512], P(None, 'blk', 'grp')
All inputs are finite; a program needn't handle non-finite values.
Results may differ from a plain program's by a relative error of at most 0.0027.
Values may be sent and summed in bfloat16 or wider, within the bound.
A program may use at most 128 MiB of HBM per device.

v0:
```python
import jax
import jax.numpy as jnp
from jax import lax
from jax.sharding import PartitionSpec as P


def solve_blocks(inverse, resid):
    width = inverse.shape[1]
    count = inverse.shape[0] // width
    blocks = inverse.reshape(count, width, width)
    parts = resid.reshape(count, width, resid.shape[1])
    value = jnp.einsum(
        "nab,nbc->nac",
        blocks,
        parts,
        precision=lax.Precision.HIGHEST,
        preferred_element_type=jnp.float32,
    )
    return value.reshape(resid.shape)


def local(factors, lower_inverse, upper_inverse, right_side):
    lower_whole = lax.all_gather(factors[0], "grp", axis=1, tiled=True)
    forward_first = solve_blocks(lower_inverse[0], right_side[0])
    low = forward_first.astype(jnp.bfloat16)
    columns = lower_whole
    coupling = jnp.dot(
        columns, lax.all_gather(low, "blk", axis=0, tiled=True), preferred_element_type=jnp.float32
    )
    forward_second = solve_blocks(lower_inverse[1], right_side[1] - coupling)
    second = solve_blocks(upper_inverse[1], forward_second)
    high = second.astype(jnp.bfloat16)
    upper_whole = lax.all_gather(factors[1], "grp", axis=1, tiled=True)
    columns = upper_whole
    coupling = jnp.dot(
        columns, lax.all_gather(high, "blk", axis=0, tiled=True), preferred_element_type=jnp.float32
    )
    first = solve_blocks(upper_inverse[0], forward_first - coupling)
    return jnp.stack([first, second])


def solution(mesh):
    in_specs = (
        P(None, "blk", "grp"),
        P(None, "blk", None),
        P(None, "blk", None),
        P(None, "blk", "grp"),
    )
    out_specs = P(None, "blk", "grp")
    return jax.shard_map(local, mesh=mesh, in_specs=in_specs, out_specs=out_specs, check_vma=False)
```

profile of v0, /device:TPU:0, one launch (start us, length us, event | category | flops | bytes accessed | tf_op | source)
XLA Modules:
  0.0 90.9 jit_solution(13537898309061365939)
XLA Ops:
  6.5 0.0 copy-start
  6.5 0.0 copy-start.1
  6.5 0.0 all-gather.5.cloned.1.call-start
  6.5 2.4 %fusion.16 = (bf16[1,384,768]{2,1,0:T(8,128)(2,1)}, bf16[1,384,768]{2,1,0:T(8,128)(2,1)}) fusion(bf16[2,384,768]{2,1,0:T(8,128)(2,1)} %param.4), kind=kLoop, calls=%fused_computation.11 | loop fusion | bytes 2359296 | tf_op jit(solution)/shard_map/slice | solution.py:33
  9.0 0.0 copy-start.2
  9.0 0.0 all-gather.5.cloned.1.call-update
  9.0 0.0 all-gather.7.cloned.1.call-start
  9.1 0.7 all-gather.7.cloned.1.call-update
  9.8 0.0 copy-done
  9.8 0.1 copy.12
  9.9 0.0 copy-done.1
  10.0 0.3 fusion.20
  10.3 0.1 copy.10
  10.5 0.0 copy-done.2
  10.5 33.8 %all_gather.12 = bf16[3072,128]{1,0:T(8,128)(2,1)S(1)} all-gather(bf16[384,128]{1,0:T(8,128)(2,1)S(1)} %bitcast_convert_fusion.1), channel_id=1, replica_groups=mesh['blk'=8,'grp'=4] {'blk'}, dimensions={0}, use_global_device_ids=true | all-gather | bytes 884736 | tf_op jit(solution)/shard_map/all_gather | solution.py:28
  44.3 0.0 all-gather.5.cloned.1.call-done
  44.3 2.8 %fusion.13 = f32[384,128]{0,1:T(8,128)S(1)} fusion(bf16[3072,128]{1,0:T(8,128)(2,1)S(1)} %all_gather.12, bf16[1,384,3072]{2,1,0:T(8,128)(2,1)} %all-gather.5.cloned.1.call-done, f32[1,384,128]{1,2,0:T(8,128)S(1)} %copy.12), kind=kOutput, calls=%fused_computation.7 | convolution fusion | flops 302039040 | bytes 3538944 | tf_op jit(solution)/shard_map/dot_general | solution.py:27
  47.1 0.1 copy.9
  47.3 0.5 fusion.21
  47.8 0.5 bitcast_convert_fusion
  48.3 32.0 %all_gather.14 = bf16[3072,128]{1,0:T(8,128)(2,1)S(1)} all-gather(bf16[384,128]{1,0:T(8,128)(2,1)S(1)} %bitcast.61), channel_id=1, replica_groups=mesh['blk'=8,'grp'=4] {'blk'}, dimensions={0}, use_global_device_ids=true | all-gather | bytes 884736 | tf_op jit(solution)/shard_map/all_gather | solution.py:36
  80.3 0.0 all-gather.7.cloned.1.call-done
  80.3 2.5 %fusion.10 = f32[384,128]{0,1:T(8,128)S(1)} fusion(f32[384,128]{0,1:T(8,128)S(1)} %copy.10, bf16[3072,128]{1,0:T(8,128)(2,1)S(1)} %all_gather.14, bf16[1,384,3072]{2,1,0:T(8,128)(2,1)} %all-gather.7.cloned.1.call-done), kind=kOutput, calls=%fused_computation.6 | convolution fusion | flops 302039040 | bytes 3538944 | tf_op jit(solution)/shard_map/dot_general | solution.py:35
  82.8 0.1 copy.11
  82.9 0.3 fusion.22
  83.3 0.8 pad_maximum_fusion
  (4 shorter events, 0.1 us)
Async XLA Ops:
  6.5 3.2 %copy-start = (f32[2,384,128]{2,1,0:T(8,128)S(1)}, f32[2,384,128]{2,1,0:T(8,128)}, u32[]{:S(2)}) copy-start(f32[2,384,128]{2,1,0:T(8,128)} %param.7) | copy-start | bytes 1179652
  6.5 3.4 %copy-start.1 = (f32[2,384,128]{2,1,0:T(8,128)S(1)}, f32[2,384,128]{2,1,0:T(8,128)}, u32[]{:S(2)}) copy-start(f32[2,384,128]{2,1,0:T(8,128)} %param.5) | copy-start | bytes 1179652
  6.5 37.8 %all-gather.5.cloned.1.call-start = ((), (), s32[]{:S(2)}) async-start(), calls=%async_computation | async-start | bytes 2949120 | tf_op jit(solution)/shard_map/all_gather | solution.py:23
  9.0 1.5 %copy-start.2 = (f32[2,384,128]{2,1,0:T(8,128)S(1)}, f32[2,384,128]{2,1,0:T(8,128)}, u32[]{:S(2)}) copy-start(f32[2,384,128]{2,1,0:T(8,128)} %param.6) | copy-start | bytes 1179652
  9.0 71.3 %all-gather.7.cloned.1.call-start = ((), (), s32[]{:S(2)}) async-start(), calls=%async_computation.1 | async-start | bytes 2949120 | tf_op jit(solution)/shard_map/all_gather | solution.py:33
Sparse Core Ops, SparseCore 0:
  9.1 26.7 all-gather.4
  37.5 24.0 all-gather.6
where the time goes:
time: 91.1 us; the launch traced here: 90.9 us
  blocking collectives  65.8 us (72%)
  between operations  13.5 us (15%)
  matrix products  6.98 us (8%)
  local copies, waits for them, and re-layouts  3.04 us (3%)
    all_gather x1, blocking collectives, local(): lax.all_gather(low, 'blk', axis=0, tiled=True)  33.8 us
    all_gather x1, blocking collectives, local(): lax.all_gather(high, 'blk', axis=0, tiled=True)  32 us
    dot_general x1, matrix products, local(): jnp.dot(columns, lax.all_gather(low, 'blk', axis=0, tiled=True), preferre...  2.78 us
    dot_general x1, matrix products, local(): jnp.dot(columns, lax.all_gather(high, 'blk', axis=0, tiled=True), preferr...  2.5 us
    slice x1, local copies, waits for them, and re-layouts, local(): upper_whole = lax.all_gather(factors[1], 'grp', axis=1, tiled=True)  2.44 us
  transfers between devices with their start and end apart: 2, of which 0 were waited for; matrix products, arithmetic and copies ran while one was open for 5% of the time, Pallas kernels for 0%

commit v1 on v0

v1 whole, which is shorter than its diff:
```python
import functools

import jax
import jax.numpy as jnp
from jax import lax
from jax.experimental import pallas as pl
from jax.experimental.pallas import tpu as pltpu
from jax.sharding import PartitionSpec as P

MESH = pl.DeviceIdType.MESH
CHUNKS = 2


def solve(inverse, resid, width):
    parts = [
        jnp.dot(
            inverse[n * width : (n + 1) * width],
            resid[n * width : (n + 1) * width],
            precision=lax.Precision.HIGHEST,
            preferred_element_type=jnp.float32,
        )
        for n in range(inverse.shape[0] // width)
    ]
    return jnp.concatenate(parts, axis=0)


def compose(left, right, width):
    return solve(left, right, width)


def kernel(nb, f, dinv, einv, rhs, out, fg, low, high, fwd, both, g_send, g_recv, f_send, f_recv):
    b, g = lax.axis_index("blk"), lax.axis_index("grp")
    width = dinv.shape[2]
    rows, depth = f.shape[1], f.shape[2]
    per = depth // rows
    line = nb // 2
    piece = rows // CHUNKS

    barrier = pltpu.get_barrier_semaphore()
    for d in range(1, line):
        pl.semaphore_signal(barrier, inc=1, device_id={"blk": b ^ (2 * d)}, device_id_type=MESH)
    pl.semaphore_signal(barrier, inc=1, device_id={"blk": b ^ 1}, device_id_type=MESH)
    for s in (1, 2):
        pl.semaphore_signal(barrier, inc=1, device_id={"grp": g ^ s}, device_id_type=MESH)

    first = solve(dinv[0], rhs[0], width)
    fwd[...] = first
    low[b] = first.astype(jnp.bfloat16)
    pl.semaphore_wait(barrier, line + 2)

    def block_copy(buf, layer, source, slot, peer):
        return pltpu.make_async_remote_copy(
            src_ref=buf.at[source],
            dst_ref=buf.at[source],
            send_sem=g_send.at[layer, slot],
            recv_sem=g_recv.at[layer, source],
            device_id={"blk": peer},
            device_id_type=MESH,
        )

    def gather_start(buf, layer):
        block_copy(buf, layer, b, 0, b ^ 1).start()
        for d in range(1, line):
            block_copy(buf, layer, b, d, b ^ (2 * d)).start()

    def gather_forward(buf, layer):
        for d in range(1, line):
            source = b ^ (2 * d)
            block_copy(buf, layer, source, 0, b ^ 1).wait_recv()
            block_copy(buf, layer, source, line - 1 + d, b ^ 1).start()

    def gather_wait(buf, layer):
        for d in range(line):
            block_copy(buf, layer, b ^ (2 * d) ^ 1, 0, b ^ 1).wait_recv()

    def gather_drain(buf, layer):
        for slot in range(2 * line - 1):
            block_copy(buf, layer, b, slot, b ^ 1).wait_send()

    def near(layer):
        return pltpu.make_async_remote_copy(
            src_ref=f.at[layer],
            dst_ref=fg.at[layer, 0],
            send_sem=f_send.at[layer, 2 * CHUNKS],
            recv_sem=f_recv.at[layer, 2 * CHUNKS],
            device_id={"grp": g ^ 1},
            device_id_type=MESH,
        )

    def across(layer, i):
        return pltpu.make_async_remote_copy(
            src_ref=f.at[layer, pl.ds(i * piece, piece)],
            dst_ref=fg.at[layer, 1, pl.ds(i * piece, piece)],
            send_sem=f_send.at[layer, i],
            recv_sem=f_recv.at[layer, i],
            device_id={"grp": g ^ 2},
            device_id_type=MESH,
        )

    def onward(layer, i):
        return pltpu.make_async_remote_copy(
            src_ref=fg.at[layer, 1, pl.ds(i * piece, piece)],
            dst_ref=fg.at[layer, 2, pl.ds(i * piece, piece)],
            send_sem=f_send.at[layer, CHUNKS + i],
            recv_sem=f_recv.at[layer, CHUNKS + i],
            device_id={"grp": g ^ 1},
            device_id_type=MESH,
        )

    def factor_forward(layer):
        for i in range(CHUNKS):
            across(layer, i).wait_recv()
            onward(layer, i).start()

    def factor_wait(layer):
        near(layer).wait_recv()
        for i in range(CHUNKS):
            onward(layer, i).wait_recv()

    def factor_drain(layer):
        near(layer).wait_send()
        for i in range(CHUNKS):
            onward(layer, i).wait_send()

    def couple(buf, layer):
        total = jnp.zeros((rows, buf.shape[2]), jnp.float32)
        for s in range(4):
            part = f.at[layer] if s == 0 else fg.at[layer, s - 1]
            start = (g ^ s) * per

            def step(j, total):
                at = pl.multiple_of(j * rows, rows)
                return total + jnp.dot(part[:, pl.ds(at, rows)], buf[start + j], preferred_element_type=jnp.float32)

            if per <= 4:
                for j in range(per):
                    total = step(j, total)
            else:
                total = lax.fori_loop(0, per, step, total)
        return total

    gather_start(low, 0)
    near(0).start()
    for i in range(CHUNKS):
        across(0, i).start()
    near(1).start()
    both[...] = compose(einv[1], dinv[1], width)
    gather_forward(low, 0)
    factor_forward(0)
    for i in range(CHUNKS):
        across(0, i).wait_send()
    for i in range(CHUNKS):
        across(1, i).start()
    gather_wait(low, 0)
    factor_wait(0)
    second = solve(both[...], rhs[1] - couple(low, 0), width)
    high[b] = second.astype(jnp.bfloat16)
    gather_start(high, 1)
    out[1] = second
    gather_drain(low, 0)
    factor_drain(0)
    gather_forward(high, 1)
    factor_forward(1)
    gather_wait(high, 1)
    factor_wait(1)
    out[0] = solve(einv[0], fwd[...] - couple(high, 1), width)
    gather_drain(high, 1)
    factor_drain(1)
    for i in range(CHUNKS):
        across(1, i).wait_send()


def solution(mesh):
    nb, ng = mesh.shape["blk"], mesh.shape["grp"]
    assert ng == 4 and nb & (nb - 1) == 0

    def local(factors, lower_inverse, upper_inverse, right_side):
        layers, rows, depth = factors.shape
        columns = right_side.shape[2]
        whole = pl.BlockSpec(memory_space=pltpu.VMEM)
        held = factors.size * 2 * 4 + nb * rows * columns * 4
        return pl.pallas_call(
            functools.partial(kernel, nb),
            out_shape=jax.ShapeDtypeStruct(right_side.shape, jnp.float32),
            in_specs=[whole] * 4,
            out_specs=whole,
            scratch_shapes=[
                pltpu.VMEM((layers, 3, rows, depth), jnp.bfloat16),
                pltpu.VMEM((nb, rows, columns), jnp.bfloat16),
                pltpu.VMEM((nb, rows, columns), jnp.bfloat16),
                pltpu.VMEM((rows, columns), jnp.float32),
                pltpu.VMEM(lower_inverse.shape[1:], jnp.float32),
                pltpu.SemaphoreType.DMA((layers, nb)),
                pltpu.SemaphoreType.DMA((layers, nb)),
                pltpu.SemaphoreType.DMA((layers, 2 * CHUNKS + 1)),
                pltpu.SemaphoreType.DMA((layers, 2 * CHUNKS + 1)),
            ],
            compiler_params=pltpu.CompilerParams(
                collective_id=0, has_side_effects=True, vmem_limit_bytes=held + 8 * 2**20
            ),
        )(factors, lower_inverse, upper_inverse, right_side)

    in_specs = (
        P(None, "blk", "grp"),
        P(None, "blk", None),
        P(None, "blk", None),
        P(None, "blk", "grp"),
    )
    return jax.shard_map(local, mesh=mesh, in_specs=in_specs, out_specs=P(None, "blk", "grp"), check_vma=False)
```

time: 91.1 us -> 42.7 us (0.47)
  blocking collectives: 65.8 us -> 0 us
  Pallas kernels: 0 us -> 37.4 us
  between operations: 13.5 us -> 0.01 us
  matrix products: 6.98 us -> 0 us
  local copies, waits for them, and re-layouts: 3.04 us -> 5 us
    all_gather x2 -> x0, blocking collectives: 65.8 us -> none  [the longest x1 33.8 us: local(): lax.all_gather(low, 'blk', axis=0, tiled=True)]
    pallas_call x0 -> x1, Pallas kernels: none -> 37.4 us  [local(): pl.pallas_call(functools.partial(kernel, nb), out_shape=jax.ShapeDtypeStr...]
    dot_general x6 -> x0, matrix products: 6.98 us -> none  [the longest x1 2.78 us: local(): jnp.dot(columns, lax.all_gather(low, 'blk', axis=0, tiled=True), preferre...]
    unnamed x7 -> x9, local copies, waits for them, and re-layouts: 0.14 us -> 5 us
    slice x4 -> x0, local copies, waits for them, and re-layouts: 2.53 us -> none  [the longest x1 2.44 us: local(): upper_whole = lax.all_gather(factors[1], 'grp', axis=1, tiled=True)]
  transfers between devices with their start and end apart: 2 -> 0, of which waited for: 0 -> 0; matrix products, arithmetic and copies ran while one was open for 5% -> 0% of each run, Pallas kernels for 0% -> 0%
where the time goes in v1:
time: 42.7 us; the launch traced here: 42.4 us
  Pallas kernels  37.4 us (88%)
  local copies, waits for them, and re-layouts  5 us (12%)
    pallas_call x1, Pallas kernels, local(): pl.pallas_call(functools.partial(kernel, nb), out_shape=jax.ShapeDtypeStr...  37.4 us
    unnamed x9, local copies, waits for them, and re-layouts  5 us

profile of v1, /device:TPU:0, one launch (start us, length us, event | category | flops | bytes accessed | tf_op | source)
XLA Modules:
  0.0 42.4 jit_solution(5790883148752062737)
XLA Ops:
  0.0 0.0 copy-start
  0.0 1.3 %copy-done = bf16[2,384,768]{2,1,0:T(8,128)(2,1)S(1)} copy-done((bf16[2,384,768]{2,1,0:T(8,128)(2,1)S(1)}, bf16[2,384,768]{2,1,0:T(8,128)(2,1)}, u32[]{:S(2)}) %copy-start) | copy-done | bytes 1179672
  1.3 0.0 copy-start.1
  1.3 1.0 %copy-done.1 = f32[2,384,128]{2,1,0:T(8,128)S(1)} copy-done((f32[2,384,128]{2,1,0:T(8,128)S(1)}, f32[2,384,128]{2,1,0:T(8,128)}, u32[]{:S(2)}) %copy-start.1) | copy-done | bytes 393240
  2.3 0.0 copy-start.2
  2.3 1.0 %copy-done.2 = f32[2,384,128]{2,1,0:T(8,128)S(1)} copy-done((f32[2,384,128]{2,1,0:T(8,128)S(1)}, f32[2,384,128]{2,1,0:T(8,128)}, u32[]{:S(2)}) %copy-start.2) | copy-done | bytes 393240
  3.3 0.0 copy-start.3
  3.3 1.0 %copy-done.3 = f32[2,384,128]{2,1,0:T(8,128)S(1)} copy-done((f32[2,384,128]{2,1,0:T(8,128)S(1)}, f32[2,384,128]{2,1,0:T(8,128)}, u32[]{:S(2)}) %copy-start.3) | copy-done | bytes 393240
  4.3 37.4 %shard_map.46 = f32[2,384,128]{2,1,0:T(8,128)S(1)} custom-call(bf16[2,384,768]{2,1,0:T(8,128)(2,1)S(1)} %copy-done, f32[2,384,128]{2,1,0:T(8,128)S(1)} %copy-done.1, f32[2,384,128]{2,1,0:T(8,128)S(1)} %copy-done.2, f32[2,384,128]{2,1,0:T(8,128)S(1)} %copy-done.3), custom_call_target="tpu_custom_call" | custom-call | tf_op jit(solution)/shard_map/pallas_call | solution.py:182
  41.6 0.7 %copy.6 = f32[2,384,128]{2,1,0:T(8,128)} copy(f32[2,384,128]{2,1,0:T(8,128)S(1)} %shard_map.46) | data formatting | bytes 786432
Async XLA Ops:
  0.0 1.3 %copy-start = (bf16[2,384,768]{2,1,0:T(8,128)(2,1)S(1)}, bf16[2,384,768]{2,1,0:T(8,128)(2,1)}, u32[]{:S(2)}) copy-start(bf16[2,384,768]{2,1,0:T(8,128)(2,1)} %f.1) | copy-start | bytes 3538948
  1.3 1.0 %copy-start.1 = (f32[2,384,128]{2,1,0:T(8,128)S(1)}, f32[2,384,128]{2,1,0:T(8,128)}, u32[]{:S(2)}) copy-start(f32[2,384,128]{2,1,0:T(8,128)} %dinv.1) | copy-start | bytes 1179652
  2.3 1.0 %copy-start.2 = (f32[2,384,128]{2,1,0:T(8,128)S(1)}, f32[2,384,128]{2,1,0:T(8,128)}, u32[]{:S(2)}) copy-start(f32[2,384,128]{2,1,0:T(8,128)} %einv.1) | copy-start | bytes 1179652
  3.3 1.0 %copy-start.3 = (f32[2,384,128]{2,1,0:T(8,128)S(1)}, f32[2,384,128]{2,1,0:T(8,128)}, u32[]{:S(2)}) copy-start(f32[2,384,128]{2,1,0:T(8,128)} %rhs.1) | copy-start | bytes 1179652

commit v2 on v1

v2 whole, which is shorter than its diff:
```python
import functools

import jax
import jax.numpy as jnp
from jax import lax
from jax.experimental import pallas as pl
from jax.experimental.pallas import tpu as pltpu
from jax.sharding import PartitionSpec as P

MESH = pl.DeviceIdType.MESH


def solve(inverse, resid, width):
    parts = [
        jnp.dot(
            inverse[n * width : (n + 1) * width],
            resid[n * width : (n + 1) * width],
            precision=lax.Precision.HIGHEST,
            preferred_element_type=jnp.float32,
        )
        for n in range(inverse.shape[0] // width)
    ]
    return jnp.concatenate(parts, axis=0)


def kernel(
    nb, f_hbm, dinv_hbm, einv_hbm, rhs_hbm, out,
    dinv, einv, rhs, fg, low, high, fwd, both, l_sem, g_send, g_recv, f_send, f_recv,
):
    b, g = lax.axis_index("blk"), lax.axis_index("grp")
    width = dinv.shape[2]
    rows, depth = fg.shape[2], fg.shape[3]
    per = depth // rows
    line = nb // 2
    at, side = b // 2, b % 2
    pieces, piece = rows // width, width

    barrier = pltpu.get_barrier_semaphore()

    def greet(**device):
        pl.semaphore_signal(barrier, inc=1, device_id=device, device_id_type=MESH)

    greet(blk=b ^ 1)
    greet(grp=g ^ 1)
    greet(grp=g ^ 2)

    greet(blk=(b + 2) % nb)
    greet(blk=(b + nb - 2) % nb)

    def load(i):
        source, target = (
            (dinv_hbm, dinv),
            (rhs_hbm, rhs),
            (einv_hbm, einv),
            (f_hbm.at[0], fg.at[0, 0]),
            (f_hbm.at[1], fg.at[1, 0]),
        )[i]
        return pltpu.make_async_copy(source, target, l_sem.at[i])

    for i in range(5):
        load(i).start()
    load(0).wait()
    load(1).wait()
    first = solve(dinv[0], rhs[0], width)
    fwd[...] = first
    low[b] = first.astype(jnp.bfloat16)
    pl.semaphore_wait(barrier, 5)

    def block_copy(buf, layer, source, way, half):
        peer = (b + 2, b - 2, b ^ 1)[way]
        window = pl.ds(half * piece, piece)
        return pltpu.make_async_remote_copy(
            src_ref=buf.at[source, window],
            dst_ref=buf.at[source, window],
            send_sem=g_send.at[layer, source, way, half],
            recv_sem=g_recv.at[layer, source, half],
            device_id={"blk": peer},
            device_id_type=MESH,
        )

    def onwards(buf, layer, source, half, ways, act):
        for way in ways:
            if way == 2:
                act(block_copy(buf, layer, source, way, half))
            else:
                @pl.when(at < line - 1 if way == 0 else at > 0)
                def _():
                    act(block_copy(buf, layer, source, way, half))

    def start(copy):
        copy.start()

    def gather_start(buf, layer, half):
        onwards(buf, layer, b, half, (0, 1, 2), start)

    def gather_forward(buf, layer, k, half):
        for way, there in ((0, at >= k), (1, at + k < line)):
            @pl.when(there)
            def _():
                source = b - 2 * k if way == 0 else b + 2 * k
                block_copy(buf, layer, source, 2, half).wait_recv()
                onwards(buf, layer, source, half, (way, 2), start)

    def gather_pass(buf, layer):
        def hop(k):
            for half in range(pieces):
                gather_forward(buf, layer, k, half)

        each(1, line, hop)

    def gather_wait(buf, layer, source):
        for half in range(pieces):
            block_copy(buf, layer, source, 2, half).wait_recv()

    def gather_drain(buf, layer):
        for half in range(pieces):
            onwards(buf, layer, b, half, (0, 1, 2), lambda copy: copy.wait_send())

            def step(k):
                for way, there in ((0, at >= k), (1, at + k < line)):
                    @pl.when(there)
                    def _():
                        source = b - 2 * k if way == 0 else b + 2 * k
                        onwards(buf, layer, source, half, (way, 2), lambda copy: copy.wait_send())

            each(1, line, step)

    def each(low_end, high_end, step):
        if high_end - low_end <= 8:
            for k in range(low_end, high_end):
                step(k)
        else:
            pl.loop(low_end, high_end)(step)

    def factor_copy(layer, source, target, slot, peer, i=None):
        if i is not None:
            source = source.at[pl.ds(i * piece, piece)]
            target = target.at[pl.ds(i * piece, piece)]
        return pltpu.make_async_remote_copy(
            src_ref=source,
            dst_ref=target,
            send_sem=f_send.at[layer, slot],
            recv_sem=f_recv.at[layer, slot],
            device_id={"grp": peer},
            device_id_type=MESH,
        )

    def near(layer):
        return factor_copy(layer, f_hbm.at[layer], fg.at[layer, 1], 2 * pieces, g ^ 1)

    def across(layer, i):
        return factor_copy(layer, f_hbm.at[layer], fg.at[layer, 2], i, g ^ 2, i)

    def onward(layer, i):
        return factor_copy(layer, fg.at[layer, 2], fg.at[layer, 3], pieces + i, g ^ 1, i)

    def factor_forward(layer, i):
        across(layer, i).wait_recv()
        onward(layer, i).start()

    def factor_drain(layer):
        near(layer).wait_send()
        for i in range(pieces):
            onward(layer, i).wait_send()

    def term(buf, layer, source):
        slot = (source // per) ^ g
        place = pl.multiple_of((source % per) * rows, rows)
        return jnp.dot(fg[layer, slot, :, pl.ds(place, rows)], buf[source], preferred_element_type=jnp.float32)

    def couple(low_end, high_end):
        window = slice(low_end, high_end)
        total = jnp.zeros((high_end - low_end, fwd.shape[1]), jnp.float32)
        for slot in range(4):
            first = (g ^ slot) * per

            def step(j, total):
                place = pl.ds(pl.multiple_of(j * rows, rows), rows)
                return total + jnp.dot(fg[0, slot, window, place], low[first + j], preferred_element_type=jnp.float32)

            if per <= 4:
                for j in range(per):
                    total = step(j, total)
            else:
                total = lax.fori_loop(0, per, step, total)
        return total

    def advance(first, last):
        for i in range(first, last):
            onward(0, i).wait_recv()
        window = slice(first * piece, last * piece)
        second = solve(both[window], rhs[1, window] - couple(first * piece, last * piece), width)
        high[b, window] = second.astype(jnp.bfloat16)
        for i in range(first, last):
            gather_start(high, 1, i)
        out[1, window] = second

    for i in range(pieces):
        across(0, i).start()
    for i in range(pieces):
        gather_start(low, 0, i)
    near(0).start()
    load(2).wait()
    both[...] = solve(einv[1], dinv[1], width)
    gather_pass(low, 0)
    near(1).start()
    for i in range(pieces - 1):
        factor_forward(0, i)
    for i in range(pieces):
        across(1, i).start()
    each(0, nb // 2, lambda k: gather_wait(low, 0, 2 * k + 1 - side))
    load(3).wait()
    near(0).wait_recv()
    advance(0, pieces - 1)
    factor_forward(0, pieces - 1)
    advance(pieces - 1, pieces)
    gather_pass(high, 1)
    for i in range(pieces):
        factor_forward(1, i)
    near(1).wait_recv()
    for i in range(pieces):
        onward(1, i).wait_recv()
    load(4).wait()
    for i in range(pieces):
        across(0, i).wait_send()
    gather_drain(low, 0)
    factor_drain(0)
    total = jnp.zeros(fwd.shape, jnp.float32)

    def mine(k, total):
        return total + term(high, 1, 2 * k + side)

    def theirs(k, total):
        source = b ^ 1 ^ (2 * k)
        gather_wait(high, 1, source)
        return total + term(high, 1, source)

    if line <= 8:
        for k in range(line):
            total = mine(k, total)
        for k in range(line):
            total = theirs(k, total)
    else:
        total = lax.fori_loop(0, line, mine, total)
        total = lax.fori_loop(0, line, theirs, total)
    out[0] = solve(einv[0], fwd[...] - total, width)
    gather_drain(high, 1)
    factor_drain(1)
    for i in range(pieces):
        across(1, i).wait_send()


def solution(mesh):
    nb, ng = mesh.shape["blk"], mesh.shape["grp"]
    assert ng == 4 and nb & (nb - 1) == 0

    def local(factors, lower_inverse, upper_inverse, right_side):
        layers, rows, depth = factors.shape
        columns = right_side.shape[2]
        whole = pl.BlockSpec(memory_space=pltpu.VMEM)
        apart = pl.BlockSpec(memory_space=pltpu.HBM)
        pieces = rows // lower_inverse.shape[2]
        held = factors.size * 2 * 4 + nb * rows * columns * 4
        return pl.pallas_call(
            functools.partial(kernel, nb),
            out_shape=jax.ShapeDtypeStruct(right_side.shape, jnp.float32),
            in_specs=[apart] * 4,
            out_specs=whole,
            scratch_shapes=[
                pltpu.VMEM(lower_inverse.shape, jnp.float32),
                pltpu.VMEM(upper_inverse.shape, jnp.float32),
                pltpu.VMEM(right_side.shape, jnp.float32),
                pltpu.VMEM((layers, 4, rows, depth), jnp.bfloat16),
                pltpu.VMEM((nb, rows, columns), jnp.bfloat16),
                pltpu.VMEM((nb, rows, columns), jnp.bfloat16),
                pltpu.VMEM((rows, columns), jnp.float32),
                pltpu.VMEM(lower_inverse.shape[1:], jnp.float32),
                pltpu.SemaphoreType.DMA((5,)),
                pltpu.SemaphoreType.DMA((layers, nb, 3, pieces)),
                pltpu.SemaphoreType.DMA((layers, nb, pieces)),
                pltpu.SemaphoreType.DMA((layers, 2 * pieces + 1)),
                pltpu.SemaphoreType.DMA((layers, 2 * pieces + 1)),
            ],
            compiler_params=pltpu.CompilerParams(
                collective_id=0, has_side_effects=True, vmem_limit_bytes=held + 8 * 2**20
            ),
        )(factors, lower_inverse, upper_inverse, right_side)

    in_specs = (
        P(None, "blk", "grp"),
        P(None, "blk", None),
        P(None, "blk", None),
        P(None, "blk", "grp"),
    )
    return jax.shard_map(local, mesh=mesh, in_specs=in_specs, out_specs=P(None, "blk", "grp"), check_vma=False)
```

time: 42.7 us -> 42.5 us (level)
  the two profiles are of different devices: /device:TPU:0 before, /device:TPU:1 now
where the time goes in v2:
time: 42.5 us; the launch traced here: 42.2 us
  Pallas kernels  37.2 us (88%)
  local copies, waits for them, and re-layouts  5 us (12%)
    pallas_call x1, Pallas kernels, local(): pl.pallas_call(functools.partial(kernel, nb), out_shape=jax.ShapeDtypeStr...  37.2 us
    unnamed x9, local copies, waits for them, and re-layouts  5 us

profile of v2, /device:TPU:1, one launch (start us, length us, event | category | flops | bytes accessed | tf_op | source)
XLA Modules:
  0.0 42.2 jit_solution(16791423718543544191)
XLA Ops:
  0.0 0.0 copy-start
  0.0 1.3 %copy-done = bf16[2,384,768]{2,1,0:T(8,128)(2,1)S(1)} copy-done((bf16[2,384,768]{2,1,0:T(8,128)(2,1)S(1)}, bf16[2,384,768]{2,1,0:T(8,128)(2,1)}, u32[]{:S(2)}) %copy-start) | copy-done | bytes 1179672
  1.3 0.0 copy-start.1
  1.3 1.0 %copy-done.1 = f32[2,384,128]{2,1,0:T(8,128)S(1)} copy-done((f32[2,384,128]{2,1,0:T(8,128)S(1)}, f32[2,384,128]{2,1,0:T(8,128)}, u32[]{:S(2)}) %copy-start.1) | copy-done | bytes 393240
  2.3 0.0 copy-start.2
  2.3 1.0 %copy-done.2 = f32[2,384,128]{2,1,0:T(8,128)S(1)} copy-done((f32[2,384,128]{2,1,0:T(8,128)S(1)}, f32[2,384,128]{2,1,0:T(8,128)}, u32[]{:S(2)}) %copy-start.2) | copy-done | bytes 393240
  3.3 0.0 copy-start.3
  3.3 1.0 %copy-done.3 = f32[2,384,128]{2,1,0:T(8,128)S(1)} copy-done((f32[2,384,128]{2,1,0:T(8,128)S(1)}, f32[2,384,128]{2,1,0:T(8,128)}, u32[]{:S(2)}) %copy-start.3) | copy-done | bytes 393240
  4.3 37.2 %shard_map.46 = f32[2,384,128]{2,1,0:T(8,128)S(1)} custom-call(bf16[2,384,768]{2,1,0:T(8,128)(2,1)S(1)} %copy-done, f32[2,384,128]{2,1,0:T(8,128)S(1)} %copy-done.1, f32[2,384,128]{2,1,0:T(8,128)S(1)} %copy-done.2, f32[2,384,128]{2,1,0:T(8,128)S(1)} %copy-done.3), custom_call_target="tpu_custom_call" | custom-call | tf_op jit(solution)/shard_map/pallas_call | solution.py:264
  41.4 0.7 %copy.6 = f32[2,384,128]{2,1,0:T(8,128)} copy(f32[2,384,128]{2,1,0:T(8,128)S(1)} %shard_map.46) | data formatting | bytes 786432
Async XLA Ops:
  0.0 1.3 %copy-start = (bf16[2,384,768]{2,1,0:T(8,128)(2,1)S(1)}, bf16[2,384,768]{2,1,0:T(8,128)(2,1)}, u32[]{:S(2)}) copy-start(bf16[2,384,768]{2,1,0:T(8,128)(2,1)} %f_hbm.1) | copy-start | bytes 3538948
  1.3 1.0 %copy-start.1 = (f32[2,384,128]{2,1,0:T(8,128)S(1)}, f32[2,384,128]{2,1,0:T(8,128)}, u32[]{:S(2)}) copy-start(f32[2,384,128]{2,1,0:T(8,128)} %dinv_hbm.1) | copy-start | bytes 1179652
  2.3 1.0 %copy-start.2 = (f32[2,384,128]{2,1,0:T(8,128)S(1)}, f32[2,384,128]{2,1,0:T(8,128)}, u32[]{:S(2)}) copy-start(f32[2,384,128]{2,1,0:T(8,128)} %einv_hbm.1) | copy-start | bytes 1179652
  3.3 1.0 %copy-start.3 = (f32[2,384,128]{2,1,0:T(8,128)S(1)}, f32[2,384,128]{2,1,0:T(8,128)}, u32[]{:S(2)}) copy-start(f32[2,384,128]{2,1,0:T(8,128)} %rhs_hbm.1) | copy-start | bytes 1179652

commit v3 on v2

--- a/solution.py
+++ b/solution.py
@@ -44,8 +44,13 @@
     greet(grp=g ^ 1)
     greet(grp=g ^ 2)
 
-    greet(blk=(b + 2) % nb)
-    greet(blk=(b + nb - 2) % nb)
+    @pl.when(at > 0)
+    def _():
+        greet(blk=b - 2)
+
+    @pl.when(at < line - 1)
+    def _():
+        greet(blk=b + 2)
 
     def load(i):
         source, target = (
@@ -64,7 +69,7 @@
     first = solve(dinv[0], rhs[0], width)
     fwd[...] = first
     low[b] = first.astype(jnp.bfloat16)
-    pl.semaphore_wait(barrier, 5)
+    pl.semaphore_wait(barrier, 3 + jnp.int32(at > 0) + jnp.int32(at < line - 1))
 
     def block_copy(buf, layer, source, way, half):
         peer = (b + 2, b - 2, b ^ 1)[way]
@@ -221,10 +226,6 @@
     for i in range(pieces):
         onward(1, i).wait_recv()
     load(4).wait()
-    for i in range(pieces):
-        across(0, i).wait_send()
-    gather_drain(low, 0)
-    factor_drain(0)
     total = jnp.zeros(fwd.shape, jnp.float32)
 
     def mine(k, total):
@@ -244,6 +245,10 @@
         total = lax.fori_loop(0, line, mine, total)
         total = lax.fori_loop(0, line, theirs, total)
     out[0] = solve(einv[0], fwd[...] - total, width)
+    for i in range(pieces):
+        across(0, i).wait_send()
+    gather_drain(low, 0)
+    factor_drain(0)
     gather_drain(high, 1)
     factor_drain(1)
     for i in range(pieces):

time: 42.5 us -> 40.7 us (0.958)
  the two profiles are of different devices: /device:TPU:1 before, /device:TPU:0 now
where the time goes in v3:
time: 40.7 us; the launch traced here: 40.5 us
  Pallas kernels  35.4 us (87%)
  local copies, waits for them, and re-layouts  5 us (12%)
    pallas_call x1, Pallas kernels, local(): pl.pallas_call(functools.partial(kernel, nb), out_shape=jax.ShapeDtypeStr...  35.4 us
    unnamed x9, local copies, waits for them, and re-layouts  5 us

profile of v3, /device:TPU:0, one launch (start us, length us, event | category | flops | bytes accessed | tf_op | source)
XLA Modules:
  0.0 40.5 jit_solution(11131696433673536691)
XLA Ops:
  0.0 0.0 copy-start
  0.0 1.3 %copy-done = bf16[2,384,768]{2,1,0:T(8,128)(2,1)S(1)} copy-done((bf16[2,384,768]{2,1,0:T(8,128)(2,1)S(1)}, bf16[2,384,768]{2,1,0:T(8,128)(2,1)}, u32[]{:S(2)}) %copy-start) | copy-done | bytes 1179672
  1.3 0.0 copy-start.1
  1.3 1.0 %copy-done.1 = f32[2,384,128]{2,1,0:T(8,128)S(1)} copy-done((f32[2,384,128]{2,1,0:T(8,128)S(1)}, f32[2,384,128]{2,1,0:T(8,128)}, u32[]{:S(2)}) %copy-start.1) | copy-done | bytes 393240
  2.3 0.0 copy-start.2
  2.3 1.0 %copy-done.2 = f32[2,384,128]{2,1,0:T(8,128)S(1)} copy-done((f32[2,384,128]{2,1,0:T(8,128)S(1)}, f32[2,384,128]{2,1,0:T(8,128)}, u32[]{:S(2)}) %copy-start.2) | copy-done | bytes 393240
  3.3 0.0 copy-start.3
  3.3 1.0 %copy-done.3 = f32[2,384,128]{2,1,0:T(8,128)S(1)} copy-done((f32[2,384,128]{2,1,0:T(8,128)S(1)}, f32[2,384,128]{2,1,0:T(8,128)}, u32[]{:S(2)}) %copy-start.3) | copy-done | bytes 393240
  4.3 35.4 %shard_map.46 = f32[2,384,128]{2,1,0:T(8,128)S(1)} custom-call(bf16[2,384,768]{2,1,0:T(8,128)(2,1)S(1)} %copy-done, f32[2,384,128]{2,1,0:T(8,128)S(1)} %copy-done.1, f32[2,384,128]{2,1,0:T(8,128)S(1)} %copy-done.2, f32[2,384,128]{2,1,0:T(8,128)S(1)} %copy-done.3), custom_call_target="tpu_custom_call" | custom-call | tf_op jit(solution)/shard_map/pallas_call | solution.py:269
  39.7 0.7 %copy.6 = f32[2,384,128]{2,1,0:T(8,128)} copy(f32[2,384,128]{2,1,0:T(8,128)S(1)} %shard_map.46) | data formatting | bytes 786432
Async XLA Ops:
  0.0 1.3 %copy-start = (bf16[2,384,768]{2,1,0:T(8,128)(2,1)S(1)}, bf16[2,384,768]{2,1,0:T(8,128)(2,1)}, u32[]{:S(2)}) copy-start(bf16[2,384,768]{2,1,0:T(8,128)(2,1)} %f_hbm.1) | copy-start | bytes 3538948
  1.3 1.0 %copy-start.1 = (f32[2,384,128]{2,1,0:T(8,128)S(1)}, f32[2,384,128]{2,1,0:T(8,128)}, u32[]{:S(2)}) copy-start(f32[2,384,128]{2,1,0:T(8,128)} %dinv_hbm.1) | copy-start | bytes 1179652
  2.3 1.0 %copy-start.2 = (f32[2,384,128]{2,1,0:T(8,128)S(1)}, f32[2,384,128]{2,1,0:T(8,128)}, u32[]{:S(2)}) copy-start(f32[2,384,128]{2,1,0:T(8,128)} %einv_hbm.1) | copy-start | bytes 1179652
  3.3 1.0 %copy-start.3 = (f32[2,384,128]{2,1,0:T(8,128)S(1)}, f32[2,384,128]{2,1,0:T(8,128)}, u32[]{:S(2)}) copy-start(f32[2,384,128]{2,1,0:T(8,128)} %rhs_hbm.1) | copy-start | bytes 1179652
